TPU v7x, 512 devices: a whole 4x8x8 slice. The times are simulated.
512 devices in a mesh: dp: 32 (over y_hi, x, core), seq: 16 (over z, y_lo).
Axes of the slice: x: 4, y: 8 (y_hi: 4, y_lo: 2; y = y_hi * 2 + y_lo), z: 8, core: 2. Of those that a mesh axis runs over, the one named last changes fastest.
Arguments:
- query_rows: bfloat16 [32, 2048, 2048], P('dp', 'seq'), may hold values from -108 to 108
- key_rows: bfloat16 [32, 2048, 2048], P('dp', 'seq'), may hold values from -6 to 6
- value_rows: bfloat16 [32, 2048, 2048], P('dp', 'seq'), may hold values from -6 to 6
- out_weight: bfloat16 [2048, 2048], P('seq', 'dp'), may hold values from -0.125 to 0.125
- grad_out: bfloat16 [32, 2048, 2048], P('dp', 'seq'), may hold values from -6 to 6
- block_list: int32 [32, 32, 8], P('dp'), may hold values from 0 to 31, as said below
Outputs:
- attended: bfloat16 [32, 2048, 2048], P('dp', 'seq')
- query_gradient: bfloat16 [32, 2048, 2048], P('dp', 'seq')
- grad_key: bfloat16 [32, 2048, 2048], P('dp', 'seq')
- grad_value: bfloat16 [32, 2048, 2048], P('dp', 'seq')
- grad_weight: float32 [2048, 2048], P('seq', 'dp')
Inputs may be any that keep to these rules, and one draw needn't show every extreme that they name: `block_list`: for query block b, slots 0 to 2 hold b - 1, b, b + 1 modulo 32, slots 3 and 4 hold 0 and 31, slots 5 to 7 are drawn at random; the same list serves all heads.
All inputs are finite; a program needn't handle non-finite values.
Results may differ from a plain program's by a relative error of at most 0.0075.
Values may be sent and summed in bfloat16 or wider, within the bound.
A program may use at most 128 MiB of HBM per device.

v0:
```python
import math
import jax
import jax.numpy as jnp
from jax import lax
from jax.sharding import PartitionSpec as P

HEAD_SIZE = 128


def spread_weight(weight_sum):
    return lax.psum_scatter(weight_sum, "dp", scatter_dimension=1, tiled=True)


def local(query_rows, key_rows, value_rows, out_weight, grad_out, block_list):
    query_all, key_all, value_all = (
        lax.all_to_all(query_rows, "seq", split_axis=2, concat_axis=1, tiled=True),
        lax.all_to_all(key_rows, "seq", split_axis=2, concat_axis=1, tiled=True),
        lax.all_to_all(value_rows, "seq", split_axis=2, concat_axis=1, tiled=True),
    )
    length = query_all.shape[1]
    width_here = query_all.shape[2]
    heads_here = width_here // HEAD_SIZE
    block_ids = block_list[0]
    block_count = block_ids.shape[0]
    slot_count = block_ids.shape[1]
    block_size = length // block_count
    logit_scale = 1.0 / math.sqrt(HEAD_SIZE)

    def to_heads(flat):
        split = flat.reshape(length, heads_here, HEAD_SIZE).transpose(1, 0, 2)
        return split.reshape(heads_here, block_count, block_size, HEAD_SIZE)

    def to_flat(blocked):
        joined = blocked.reshape(heads_here, length, HEAD_SIZE).transpose(1, 0, 2)
        return joined.reshape(1, length, width_here)

    blocked_queries = to_heads(query_all[0])
    key_block_indices = to_heads(key_all[0])[:, block_ids].reshape(
        heads_here, block_count, slot_count * block_size, HEAD_SIZE
    )
    value_block_indices = to_heads(value_all[0])[:, block_ids].reshape(
        heads_here, block_count, slot_count * block_size, HEAD_SIZE
    )
    attention_logits = (
        jnp.einsum(
            "hbqd,hbkd->hbqk",
            blocked_queries,
            key_block_indices,
            preferred_element_type=jnp.float32,
        )
        * logit_scale
    )
    highest = jnp.max(attention_logits, axis=-1, keepdims=True)
    expo = jnp.exp(attention_logits - highest)
    attn_probs = expo / jnp.sum(expo, axis=-1, keepdims=True)
    reduced_probabilities = attn_probs.astype(jnp.bfloat16)
    attended = jnp.einsum(
        "hbqk,hbkd->hbqd",
        reduced_probabilities,
        value_block_indices,
        preferred_element_type=jnp.float32,
    ).astype(jnp.bfloat16)
    attended_flat = to_flat(attended)
    attended_seq = lax.all_to_all(attended_flat, "seq", split_axis=1, concat_axis=2, tiled=True)
    weight_here = lax.all_gather(out_weight, "dp", axis=1, tiled=True)
    gathered_grad = lax.all_gather(grad_out, "seq", axis=1, tiled=True)[0]
    grad_flat = lax.dot_general(
        gathered_grad, weight_here, (((1,), (1,)), ((), ())), preferred_element_type=jnp.float32
    ).astype(jnp.bfloat16)
    weight_sum = lax.dot_general(
        attended_flat[0],
        gathered_grad,
        (((0,), (0,)), ((), ())),
        preferred_element_type=jnp.float32,
    )
    weight_part = None
    gradient_per_block = to_heads(grad_flat)
    value_contributions = jnp.einsum(
        "hbqk,hbqd->hbkd",
        reduced_probabilities,
        gradient_per_block,
        preferred_element_type=jnp.float32,
    )
    probability_gradient = jnp.einsum(
        "hbqd,hbkd->hbqk",
        gradient_per_block,
        value_block_indices,
        preferred_element_type=jnp.float32,
    )
    row_delta = jnp.sum(attn_probs * probability_gradient, axis=-1, keepdims=True)
    score_gradient = (attn_probs * (probability_gradient - row_delta) * logit_scale).astype(
        jnp.bfloat16
    )
    query_gradient = jnp.einsum(
        "hbqk,hbkd->hbqd", score_gradient, key_block_indices, preferred_element_type=jnp.float32
    ).astype(jnp.bfloat16)
    key_contributions = jnp.einsum(
        "hbqk,hbqd->hbkd", score_gradient, blocked_queries, preferred_element_type=jnp.float32
    )
    one_hot = (
        block_ids[:, :, None] == jnp.arange(block_count, dtype=jnp.int32)[None, None, :]
    ).astype(jnp.float32)

    def collect(terms):
        spread = terms.reshape(heads_here, block_count, slot_count, block_size * HEAD_SIZE)
        summed = jnp.einsum(
            "hqsx,qsk->hkx",
            spread,
            one_hot,
            precision=lax.Precision.HIGHEST,
            preferred_element_type=jnp.float32,
        )
        return summed.reshape(heads_here, block_count, block_size, HEAD_SIZE).astype(jnp.bfloat16)

    grad_key = collect(key_contributions)
    grad_value = collect(value_contributions)
    weight_part = spread_weight(weight_sum)
    query_back, key_back, value_back = (
        lax.all_to_all(to_flat(query_gradient), "seq", split_axis=1, concat_axis=2, tiled=True),
        lax.all_to_all(to_flat(grad_key), "seq", split_axis=1, concat_axis=2, tiled=True),
        lax.all_to_all(to_flat(grad_value), "seq", split_axis=1, concat_axis=2, tiled=True),
    )
    return (attended_seq, query_back, key_back, value_back, weight_part)


def solution(mesh):
    return jax.shard_map(
        local,
        mesh=mesh,
        in_specs=(
            P("dp", "seq", None),
            P("dp", "seq", None),
            P("dp", "seq", None),
            P("seq", "dp"),
            P("dp", "seq", None),
            P("dp", None, None),
        ),
        out_specs=(
            P("dp", "seq", None),
            P("dp", "seq", None),
            P("dp", "seq", None),
            P("dp", "seq", None),
            P("seq", "dp"),
        ),
        check_vma=False,
    )
```

profile of v0, /device:TPU:22, one launch (start us, length us, event | category | flops | bytes accessed | tf_op | source)
XLA Modules:
  0.0 454.0 jit_solution(4954409773281861823)
XLA Ops:
  7.2 0.7 all-gather.2.cloned.1.call-update
  7.9 2.4 copy.81
  10.3 0.5 broadcast.67
  10.8 11.6 %reduce.8 = bf16[2048,128]{1,0:T(8,128)(2,1)S(1)} reduce(bf16[2048,1,128]{2,1,0:T(2,128)(2,1)S(1)} %bitcast.142, bf16[]{:T(256)} %broadcast.67), dimensions={1}, to_apply=%bitcast.91.reduce_sub_computation | reduce | bytes 1048578
  22.4 0.9 reshape.177
  23.3 11.4 %all-to-all-start.1 = ((bf16[16,2,8192]{2,1,0:T(2,128)(2,1)}), bf16[16,2,8192]{2,1,0:T(2,128)(2,1)S(1)}, u32[]{:S(2)}, u32[]{:S(2)}) async-start(bf16[16,2,8192]{2,1,0:T(2,128)(2,1)} %reshape.177), calls=%async_computation.1 | async-start | bytes 1048576 | tf_op jit(solution)/shard_map/all_to_all | solution.py:16
  34.7 0.8 copy.78
  35.5 11.5 %reduce.7 = bf16[2048,128]{1,0:T(8,128)(2,1)S(1)} reduce(bf16[2048,1,128]{2,1,0:T(2,128)(2,1)S(1)} %bitcast.146, bf16[]{:T(256)} %broadcast.67), dimensions={1}, to_apply=%bitcast.89.reduce_sub_computation | reduce | bytes 1048578
  47.1 0.9 reshape.175
  48.0 8.3 %all-to-all-done.1 = bf16[16,2,8192]{2,1,0:T(2,128)(2,1)S(1)} async-done(((bf16[16,2,8192]{2,1,0:T(2,128)(2,1)}), bf16[16,2,8192]{2,1,0:T(2,128)(2,1)S(1)}, u32[]{:S(2)}, u32[]{:S(2)}) %all-to-all-start.1) | async-done | bytes 524320 | tf_op jit(solution)/shard_map/all_to_all | solution.py:16
  56.3 14.0 %all-to-all-start = ((bf16[16,2,8192]{2,1,0:T(2,128)(2,1)}), bf16[16,2,8192]{2,1,0:T(2,128)(2,1)S(1)}, u32[]{:S(2)}, u32[]{:S(2)}) async-start(bf16[16,2,8192]{2,1,0:T(2,128)(2,1)} %reshape.175), calls=%async_computation | async-start | bytes 1048576 | tf_op jit(solution)/shard_map/all_to_all | solution.py:17
  70.3 0.8 copy.83
  71.1 11.5 %reduce.6 = bf16[2048,128]{1,0:T(8,128)(2,1)S(1)} reduce(bf16[2048,1,128]{2,1,0:T(2,128)(2,1)S(1)} %bitcast.147, bf16[]{:T(256)} %broadcast.67), dimensions={1}, to_apply=%bitcast.87.reduce_sub_computation | reduce | bytes 1048578
  82.6 0.9 reshape.173
  83.5 6.8 %all-to-all-done = bf16[16,2,8192]{2,1,0:T(2,128)(2,1)S(1)} async-done(((bf16[16,2,8192]{2,1,0:T(2,128)(2,1)}), bf16[16,2,8192]{2,1,0:T(2,128)(2,1)S(1)}, u32[]{:S(2)}, u32[]{:S(2)}) %all-to-all-start) | async-done | bytes 524320 | tf_op jit(solution)/shard_map/all_to_all | solution.py:17
  90.4 4.0 all-to-all-start.2
  94.6 51.6 %all_gather.7 = bf16[128,2048]{0,1:T(8,128)(2,1)} all-gather(bf16[128,64]{0,1:T(8,128)(2,1)S(1)} %copy-done.7), channel_id=1, replica_groups=mesh['dp'=32,'seq'=16] {'dp'}, dimensions={1}, use_global_device_ids=true | all-gather | bytes 540672 | tf_op jit(solution)/shard_map/all_gather | solution.py:65
  146.3 0.5 reshape.178
  146.9 0.3 copy.82
  147.2 0.5 reshape.176
  147.8 0.3 copy.79
  148.1 0.5 reshape.174
  149.0 3.1 gather_fusion.1
  152.1 3.1 gather_fusion
  155.1 5.8 %fusion.58 = (f32[32,64]{1,0:T(8,128)S(1)}, f32[32,64,512]{2,1,0:T(8,128)}) fusion(bf16[32,512,128]{2,1,0:T(8,128)(2,1)} %bitcast.140, bf16[32,64,128]{2,1,0:T(8,128)(2,1)S(1)} %bitcast.167), kind=kOutput, calls=%fused_computation.49 | convolution fusion | flops 271581696 | bytes 8921088 | tf_op jit(solution)/shard_map/sub | solution.py:54
  161.0 4.4 convolution_convert_fusion
  165.4 8.1 %copy.135 = bf16[1,2048,128]{2,0,1:T(2,128)(2,1)S(1)} copy(bf16[1,2048,128]{2,1,0:T(8,128)(2,1)S(1)} %bitcast.149) | data formatting | bytes 1048576 | tf_op jit(solution)/shard_map/reshape;transpose;reshape | solution.py:35
  173.5 11.9 %reduce.9 = bf16[2048,128]{1,0:T(8,128)(2,1)S(1)} reduce(bf16[2048,1,128]{2,1,0:T(2,128)(2,1)S(1)} %bitcast.148, bf16[]{:T(256)} %broadcast.67), dimensions={1}, to_apply=%bitcast.124.reduce_sub_computation | reduce | bytes 1048578
  185.5 0.9 reshape.179
  186.4 8.3 %all-to-all-start.3 = ((bf16[16,2,8192]{2,1,0:T(2,128)(2,1)}), bf16[16,2,8192]{2,1,0:T(2,128)(2,1)S(1)}, u32[]{:S(2)}, u32[]{:S(2)}) async-start(bf16[16,2,8192]{2,1,0:T(2,128)(2,1)} %reshape.179), calls=%async_computation.3 | async-start | bytes 1048576 | tf_op jit(solution)/shard_map/all_to_all | solution.py:64
  194.7 36.4 %all-gather.2.cloned.1.call-done = bf16[1,2048,2048]{2,1,0:T(8,128)(2,1)} async-done(((bf16[1,128,2048]{2,1,0:T(8,128)(2,1)}), bf16[1,2048,2048]{2,1,0:T(8,128)(2,1)}) %all-gather.2.cloned.1.call-update) | async-done | bytes 8388624 | tf_op jit(solution)/shard_map/all_gather | solution.py:66
  231.1 5.9 %fusion.18 = bf16[2048,128]{1,0:T(8,128)(2,1)S(1)} fusion(bf16[128,2048]{0,1:T(8,128)(2,1)S(1)} %copy-done.5, bf16[1,2048,2048]{2,1,0:T(8,128)(2,1)} %all-gather.2.cloned.1.call-done), kind=kOutput, calls=%fused_computation.22 | convolution fusion | flops 1074003968 | bytes 9437184 | tf_op jit(solution)/shard_map/dot_general | solution.py:67
  237.0 3.5 fusion.61
  240.6 18.6 %fusion.42 = bf16[32,64,128]{2,1,0:T(8,128)(2,1)S(1)} fusion(bf16[32,512,128]{2,1,0:T(8,128)(2,1)} %bitcast.141, f32[32,64,512]{2,1,0:T(8,128)} %fusion.61, f32[32,64,512]{2,1,0:T(8,128)} %get-tuple-element.26, f32[32,64]{1,0:T(8,128)S(1)} %get-tuple-element.25), kind=kOutput, calls=%fused_computation.34 | convolution fusion | flops 276040192 | bytes 13115392 | tf_op jit(solution)/shard_map/hbqk,hbkd->hbqd/dot_general | solution.py:94
  259.2 8.1 %copy.134 = bf16[1,2048,128]{2,0,1:T(2,128)(2,1)S(1)} copy(bf16[1,2048,128]{2,1,0:T(8,128)(2,1)S(1)} %bitcast.166) | data formatting | bytes 1048576 | tf_op jit(solution)/shard_map/reshape;transpose;reshape | solution.py:35
  267.3 11.7 %reduce.10 = bf16[2048,128]{1,0:T(8,128)(2,1)S(1)} reduce(bf16[2048,1,128]{2,1,0:T(2,128)(2,1)S(1)} %bitcast.144, bf16[]{:T(256)} %broadcast.67), dimensions={1}, to_apply=%bitcast.123.reduce_sub_computation | reduce | bytes 1048578
  279.0 0.9 reshape.181
  279.9 8.8 %all-to-all-start.4 = ((bf16[16,2,8192]{2,1,0:T(2,128)(2,1)}), bf16[16,2,8192]{2,1,0:T(2,128)(2,1)S(1)}, u32[]{:S(2)}, u32[]{:S(2)}) async-start(bf16[16,2,8192]{2,1,0:T(2,128)(2,1)} %reshape.181), calls=%async_computation.4 | async-start | bytes 1048576 | tf_op jit(solution)/shard_map/all_to_all | solution.py:119
  288.8 7.8 %fusion.2 = f32[128,2048]{0,1:T(8,128)} fusion(bf16[2048,128]{1,0:T(8,128)(2,1)S(1)} %bitcast.150, bf16[1,2048,2048]{2,1,0:T(8,128)(2,1)} %all-gather.2.cloned.1.call-done), kind=kOutput, calls=%fused_computation.6 | convolution fusion | flops 1073741824 | bytes 9961472 | tf_op jit(solution)/shard_map/dot_general | solution.py:70
  296.6 21.3 %fusion.22 = f32[32,512,128]{2,1,0:T(8,128)} fusion(bf16[32,64,128]{2,1,0:T(8,128)(2,1)S(1)} %bitcast.168, f32[32,64,512]{2,1,0:T(8,128)} %fusion.61, f32[32,64,512]{2,1,0:T(8,128)} %get-tuple-element.26, f32[32,64]{1,0:T(8,128)S(1)} %get-tuple-element.25), kind=kOutput, calls=%fused_computation.23 | convolution fusion | flops 275778048 | bytes 17309696 | tf_op jit(solution)/shard_map/hbqk,hbqd->hbkd/dot_general | solution.py:97
  317.9 9.6 %reshape.140 = f32[32,8,8192]{2,1,0:T(8,128)} reshape(f32[32,512,128]{2,1,0:T(8,128)} %fusion.22) | data formatting | bytes 16777216 | tf_op jit(solution)/shard_map/reshape.33
  327.6 5.1 %copy.131 = f32[32,8,64,128]{3,2,1,0:T(8,128)S(1)} copy(f32[32,8,64,128]{3,1,2,0:T(8,128)} %bitcast.127) | data formatting | bytes 16777216
  332.6 8.2 %fusion.39 = bf16[32,64,128]{2,0,1:T(8,128)(2,1)S(1)} fusion(f32[64,128,32,8]{1,0,3,2:T(8,128)S(1)} %bitcast.128, s32[32,8]{0,1:T(8,128)S(1)} %bitcast.169), kind=kOutput, calls=%fused_computation.32 | convolution fusion | flops 805576704 | bytes 8913920 | tf_op jit(solution)/shard_map/hqsx,qsk->hkx/dot_general | solution.py:106
  341.0 8.5 %copy.133 = bf16[1,2048,128]{2,0,1:T(2,128)(2,1)S(1)} copy(bf16[1,2048,128]{2,1,0:T(8,128)(2,1)S(1)} %bitcast.154) | data formatting | bytes 1048576 | tf_op jit(solution)/shard_map/reshape;transpose;reshape | solution.py:35
  349.6 11.5 %reduce.11 = bf16[2048,128]{1,0:T(8,128)(2,1)S(1)} reduce(bf16[2048,1,128]{2,1,0:T(2,128)(2,1)S(1)} %bitcast.145, bf16[]{:T(256)} %broadcast.67), dimensions={1}, to_apply=%bitcast.122.reduce_sub_computation | reduce | bytes 1048578
  361.1 0.9 reshape.183
  362.0 8.3 %all-to-all-start.5 = ((bf16[16,2,8192]{2,1,0:T(2,128)(2,1)}), bf16[16,2,8192]{2,1,0:T(2,128)(2,1)S(1)}, u32[]{:S(2)}, u32[]{:S(2)}) async-start(bf16[16,2,8192]{2,1,0:T(2,128)(2,1)} %reshape.183), calls=%async_computation.5 | async-start | bytes 1048576 | tf_op jit(solution)/shard_map/all_to_all | solution.py:120
  370.3 7.2 %fusion.45 = f32[32,512,128]{2,1,0:T(8,128)} fusion(bf16[32,64,128]{2,1,0:T(8,128)(2,1)S(1)} %bitcast.165, f32[32,64,512]{2,1,0:T(8,128)} %get-tuple-element.26, f32[32,64]{1,0:T(8,128)S(1)} %get-tuple-element.25), kind=kOutput, calls=%fused_computation.35 | convolution fusion | flops 270532608 | bytes 13115392 | tf_op jit(solution)/shard_map/hbqk,hbqd->hbkd/dot_general | solution.py:78
  377.5 9.4 %reshape.141 = f32[32,8,8192]{2,1,0:T(8,128)} reshape(f32[32,512,128]{2,1,0:T(8,128)} %fusion.45) | data formatting | bytes 16777216 | tf_op jit(solution)/shard_map/reshape.40
  386.9 5.0 %copy.130 = f32[32,8,64,128]{3,2,1,0:T(8,128)S(1)} copy(f32[32,8,64,128]{3,1,2,0:T(8,128)} %bitcast.129) | data formatting | bytes 16777216
  391.9 8.2 %fusion.36 = bf16[32,64,128]{2,0,1:T(8,128)(2,1)S(1)} fusion(f32[64,128,32,8]{1,0,3,2:T(8,128)S(1)} %bitcast.130, s32[32,8]{0,1:T(8,128)S(1)} %bitcast.170), kind=kOutput, calls=%fused_computation.31 | convolution fusion | flops 805576704 | bytes 8913920 | tf_op jit(solution)/shard_map/hqsx,qsk->hkx/dot_general | solution.py:106
  400.3 8.3 %copy.132 = bf16[1,2048,128]{2,0,1:T(2,128)(2,1)S(1)} copy(bf16[1,2048,128]{2,1,0:T(8,128)(2,1)S(1)} %bitcast.155) | data formatting | bytes 1048576 | tf_op jit(solution)/shard_map/reshape;transpose;reshape | solution.py:35
  408.6 11.5 %reduce.12 = bf16[2048,128]{1,0:T(8,128)(2,1)S(1)} reduce(bf16[2048,1,128]{2,1,0:T(2,128)(2,1)S(1)} %bitcast.143, bf16[]{:T(256)} %broadcast.67), dimensions={1}, to_apply=%bitcast.121.reduce_sub_computation | reduce | bytes 1048578
  420.2 0.9 reshape.185
  421.1 8.2 %all-to-all-start.6 = ((bf16[16,2,8192]{2,1,0:T(2,128)(2,1)}), bf16[16,2,8192]{2,1,0:T(2,128)(2,1)S(1)}, u32[]{:S(2)}, u32[]{:S(2)}) async-start(bf16[16,2,8192]{2,1,0:T(2,128)(2,1)} %reshape.185), calls=%async_computation.6 | async-start | bytes 1048576 | tf_op jit(solution)/shard_map/all_to_all | solution.py:121
  429.3 0.5 reshape.180
  430.2 1.0 copy.97
  431.2 0.5 reshape.182
  432.1 1.0 copy.98
  433.1 0.5 reshape.184
  434.0 1.0 copy.99
  435.0 10.0 %all-to-all-done.6 = bf16[16,2,8192]{2,1,0:T(2,128)(2,1)S(1)} async-done(((bf16[16,2,8192]{2,1,0:T(2,128)(2,1)}), bf16[16,2,8192]{2,1,0:T(2,128)(2,1)S(1)}, u32[]{:S(2)}, u32[]{:S(2)}) %all-to-all-start.6) | async-done | bytes 524320 | tf_op jit(solution)/shard_map/all_to_all | solution.py:121
  445.1 0.5 reshape.186
  445.9 1.0 copy.100
  (42 shorter events, 2.6 us)
Async XLA Ops:
  7.2 27.6 %copy-start.1 = (bf16[1,128,2048]{2,1,0:T(8,128)(2,1)S(1)}, bf16[1,128,2048]{2,1,0:T(8,128)(2,1)}, u32[]{:S(2)}) copy-start(bf16[1,128,2048]{2,1,0:T(8,128)(2,1)} %param.7) | copy-start | bytes 1572868
  7.2 224.0 %all-gather.2.cloned.1.call-start = ((), (), s32[]{:S(2)}) async-start(), calls=%async_computation.8 | async-start | bytes 8912896 | tf_op jit(solution)/shard_map/all_gather | solution.py:66
  10.8 59.5 %copy-start.2 = (bf16[1,128,2048]{2,1,0:T(8,128)(2,1)S(1)}, bf16[1,128,2048]{2,1,0:T(8,128)(2,1)}, u32[]{:S(2)}) copy-start(bf16[1,128,2048]{2,1,0:T(8,128)(2,1)} %param.8) | copy-start | bytes 1572868
  23.3 33.0 %all-to-all-start.1 = ((bf16[16,2,8192]{2,1,0:T(2,128)(2,1)}), bf16[16,2,8192]{2,1,0:T(2,128)(2,1)S(1)}, u32[]{:S(2)}, u32[]{:S(2)}) async-start(bf16[16,2,8192]{2,1,0:T(2,128)(2,1)} %reshape.177), calls=%async_computation.1 | async-start | bytes 1048576 | tf_op jit(solution)/shard_map/all_to_all | solution.py:16
  35.5 58.9 %copy-start.6 = (s32[1,32,8]{1,2,0:T(8,128)S(1)}, s32[1,32,8]{1,2,0:T(8,128)}, u32[]{:S(2)}) copy-start(s32[1,32,8]{1,2,0:T(8,128)} %param.11) | copy-start | bytes 3076
  35.5 59.1 %copy-start.7 = (bf16[128,64]{0,1:T(8,128)(2,1)S(1)}, bf16[128,64]{0,1:T(8,128)(2,1)}, u32[]{:S(2)}) copy-start(bf16[128,64]{0,1:T(8,128)(2,1)} %param.9) | copy-start | bytes 49156
  56.3 34.1 %all-to-all-start = ((bf16[16,2,8192]{2,1,0:T(2,128)(2,1)}), bf16[16,2,8192]{2,1,0:T(2,128)(2,1)S(1)}, u32[]{:S(2)}, u32[]{:S(2)}) async-start(bf16[16,2,8192]{2,1,0:T(2,128)(2,1)} %reshape.175), calls=%async_computation | async-start | bytes 1048576 | tf_op jit(solution)/shard_map/all_to_all | solution.py:17
  90.4 57.7 %all-to-all-start.2 = ((bf16[16,2,8192]{2,1,0:T(2,128)(2,1)}), bf16[16,2,8192]{2,1,0:T(2,128)(2,1)S(1)}, u32[]{:S(2)}, u32[]{:S(2)}) async-start(bf16[16,2,8192]{2,1,0:T(2,128)(2,1)} %reshape.173), calls=%async_computation.2 | async-start | bytes 1048576 | tf_op jit(solution)/shard_map/all_to_all | solution.py:18
  147.2 8.0 %copy-start.3 = (bf16[1,16,128,128]{3,2,1,0:T(8,128)(2,1)}, bf16[1,16,128,128]{3,2,1,0:T(8,128)(2,1)S(1)}, u32[]{:S(2)}) copy-start(bf16[1,16,128,128]{3,2,1,0:T(8,128)(2,1)S(1)} %copy.82) | copy-start | bytes 1572868
  165.4 65.8 %copy-start.5 = (bf16[128,2048]{0,1:T(8,128)(2,1)S(1)}, bf16[128,2048]{0,1:T(8,128)(2,1)}, u32[]{:S(2)}) copy-start(bf16[128,2048]{0,1:T(8,128)(2,1)} %all_gather.7) | copy-start | bytes 1572868
  186.4 93.5 %all-to-all-start.3 = ((bf16[16,2,8192]{2,1,0:T(2,128)(2,1)}), bf16[16,2,8192]{2,1,0:T(2,128)(2,1)S(1)}, u32[]{:S(2)}, u32[]{:S(2)}) async-start(bf16[16,2,8192]{2,1,0:T(2,128)(2,1)} %reshape.179), calls=%async_computation.3 | async-start | bytes 1048576 | tf_op jit(solution)/shard_map/all_to_all | solution.py:64
  231.1 5.9 %copy-start = (bf16[256,64,128]{2,1,0:T(8,128)(2,1)S(1)}, bf16[256,64,128]{2,1,0:T(8,128)(2,1)}, u32[]{:S(2)}) copy-start(bf16[256,64,128]{2,1,0:T(8,128)(2,1)} %gather_fusion.1) | copy-start | bytes 12582916
  279.9 82.1 %all-to-all-start.4 = ((bf16[16,2,8192]{2,1,0:T(2,128)(2,1)}), bf16[16,2,8192]{2,1,0:T(2,128)(2,1)S(1)}, u32[]{:S(2)}, u32[]{:S(2)}) async-start(bf16[16,2,8192]{2,1,0:T(2,128)(2,1)} %reshape.181), calls=%async_computation.4 | async-start | bytes 1048576 | tf_op jit(solution)/shard_map/all_to_all | solution.py:119
  288.7 158.2 %reduce-scatter.2.cloned.1.call-start = ((), (), s32[]{:S(2)}) async-start(), calls=%async_computation.9 | async-start | bytes 1081344 | tf_op jit(solution)/shard_map/reduce_scatter | solution.py:11
  288.8 7.8 %copy-start.4 = (bf16[1,16,128,128]{3,2,1,0:T(8,128)(2,1)S(1)}, bf16[1,16,128,128]{3,2,1,0:T(8,128)(2,1)}, u32[]{:S(2)}) copy-start(bf16[1,16,128,128]{3,2,1,0:T(8,128)(2,1)} %copy-done.3) | copy-start | bytes 1572868
  362.0 59.1 %all-to-all-start.5 = ((bf16[16,2,8192]{2,1,0:T(2,128)(2,1)}), bf16[16,2,8192]{2,1,0:T(2,128)(2,1)S(1)}, u32[]{:S(2)}, u32[]{:S(2)}) async-start(bf16[16,2,8192]{2,1,0:T(2,128)(2,1)} %reshape.183), calls=%async_computation.5 | async-start | bytes 1048576 | tf_op jit(solution)/shard_map/all_to_all | solution.py:120
  421.1 24.0 %all-to-all-start.6 = ((bf16[16,2,8192]{2,1,0:T(2,128)(2,1)}), bf16[16,2,8192]{2,1,0:T(2,128)(2,1)S(1)}, u32[]{:S(2)}, u32[]{:S(2)}) async-start(bf16[16,2,8192]{2,1,0:T(2,128)(2,1)} %reshape.185), calls=%async_computation.6 | async-start | bytes 1048576 | tf_op jit(solution)/shard_map/all_to_all | solution.py:121
Sparse Core Ops, SparseCore 0:
  10.1 221.0 all-gather.1
  296.7 95.7 reduce-scatter.1
where the time goes:
time: 463 us; the launch traced here: 454 us
  matrix products  90.8 us (20%)
  local copies, waits for them, and re-layouts  90 us (19%)
  other arithmetic  81.4 us (18%)
  starting transfers between devices  63.2 us (14%)
  waiting for transfers between devices  62.3 us (13%)
  blocking collectives  51.6 us (11%)
  between operations  14.7 us (3%)
    unnamed x7, other arithmetic  81.4 us
    all_gather x1, blocking collectives, local(): weight_here = lax.all_gather(out_weight, 'dp', axis=1, tiled=True)  51.6 us
    all_gather x1, waiting for transfers between devices, local(): gathered_grad = lax.all_gather(grad_out, 'seq', axis=1, tiled=True)[0]  36.4 us
    another operation x4, local copies, waits for them, and re-layouts, to_flat(): return joined.reshape(1, length, width_here)  33.2 us
    unnamed x47, local copies, waits for them, and re-layouts  29.2 us
    dot_general x1, matrix products, local(): jnp.einsum('hbqk,hbqd->hbkd', score_gradient, blocked_queries, preferred_...  21.3 us
    another operation x2, local copies, waits for them, and re-layouts  19 us
    dot_general x1, matrix products, local(): jnp.einsum('hbqk,hbkd->hbqd', score_gradient, key_block_indices, preferre...  18.6 us
  transfers between devices with their start and end apart: 9, of which 4 were waited for; matrix products, arithmetic and copies ran while one was open for 58% of the time, Pallas kernels for 0%

commit v1 on v0

--- a/solution.py
+++ b/solution.py
@@ -62,7 +62,9 @@
     ).astype(jnp.bfloat16)
     attended_flat = to_flat(attended)
     attended_seq = lax.all_to_all(attended_flat, "seq", split_axis=1, concat_axis=2, tiled=True)
-    weight_here = lax.all_gather(out_weight, "dp", axis=1, tiled=True)
+    weight_here = jnp.concatenate(
+        lax.all_to_all(jnp.stack([out_weight] * lax.axis_size("dp")), "dp", 0, 0), axis=1
+    )
     gathered_grad = lax.all_gather(grad_out, "seq", axis=1, tiled=True)[0]
     grad_flat = lax.dot_general(
         gathered_grad, weight_here, (((1,), (1,)), ((), ())), preferred_element_type=jnp.float32

time: 463 us -> 470 us (1.015)
  the two profiles are of different devices: /device:TPU:22 before, /device:TPU:40 now
where the time goes in v1:
time: 470 us; the launch traced here: 461 us
  waiting for transfers between devices  113 us (24%)
  local copies, waits for them, and re-layouts  90.6 us (19%)
  matrix products  90.2 us (19%)
  other arithmetic  81.5 us (17%)
  starting transfers between devices  70.8 us (15%)
  between operations  14.6 us (3%)
    unnamed x7, other arithmetic  81.5 us
    all_gather x1, waiting for transfers between devices, local(): gathered_grad = lax.all_gather(grad_out, 'seq', axis=1, tiled=True)[0]  80 us
    another operation x4, local copies, waits for them, and re-layouts, to_flat(): return joined.reshape(1, length, width_here)  32.9 us
    unnamed x45, local copies, waits for them, and re-layouts  29.1 us
    dot_general x1, matrix products, local(): jnp.einsum('hbqk,hbqd->hbkd', score_gradient, blocked_queries, preferred_...  20.8 us
    another operation x2, local copies, waits for them, and re-layouts  19 us
    dot_general x1, matrix products, local(): jnp.einsum('hbqk,hbkd->hbqd', score_gradient, key_block_indices, preferre...  18.6 us
    dot_general x2, matrix products, collect(): jnp.einsum('hqsx,qsk->hkx', spread, one_hot, precision=lax.Precision.HIGH...  16.3 us
  transfers between devices with their start and end apart: 10, of which 5 were waited for; matrix products, arithmetic and copies ran while one was open for 57% of the time, Pallas kernels for 0%

profile of v1, /device:TPU:40, one launch (start us, length us, event | category | flops | bytes accessed | tf_op | source)
XLA Modules:
  0.0 460.9 jit_solution(9392119995237609170)
XLA Ops:
  7.2 0.7 all-gather.2.cloned.1.call-update
  7.9 2.4 copy.82
  10.3 0.5 broadcast.69
  10.8 11.6 %reduce.8 = bf16[2048,128]{1,0:T(8,128)(2,1)S(1)} reduce(bf16[2048,1,128]{2,1,0:T(2,128)(2,1)S(1)} %bitcast.145, bf16[]{:T(256)} %broadcast.69), dimensions={1}, to_apply=%bitcast.94.reduce_sub_computation | reduce | bytes 1048578
  22.4 0.9 reshape.187
  23.3 11.8 %all-to-all-start.1 = ((bf16[16,2,8192]{2,1,0:T(2,128)(2,1)}), bf16[16,2,8192]{2,1,0:T(2,128)(2,1)S(1)}, u32[]{:S(2)}, u32[]{:S(2)}) async-start(bf16[16,2,8192]{2,1,0:T(2,128)(2,1)} %reshape.187), calls=%async_computation.1 | async-start | bytes 1048576 | tf_op jit(solution)/shard_map/all_to_all | solution.py:16
  35.1 0.8 copy.79
  35.9 11.5 %reduce.7 = bf16[2048,128]{1,0:T(8,128)(2,1)S(1)} reduce(bf16[2048,1,128]{2,1,0:T(2,128)(2,1)S(1)} %bitcast.149, bf16[]{:T(256)} %broadcast.69), dimensions={1}, to_apply=%bitcast.92.reduce_sub_computation | reduce | bytes 1048578
  47.4 0.9 reshape.185
  48.3 2.8 all-to-all-done.1
  51.1 9.7 %all-to-all-start = ((bf16[16,2,8192]{2,1,0:T(2,128)(2,1)}), bf16[16,2,8192]{2,1,0:T(2,128)(2,1)S(1)}, u32[]{:S(2)}, u32[]{:S(2)}) async-start(bf16[16,2,8192]{2,1,0:T(2,128)(2,1)} %reshape.185), calls=%async_computation | async-start | bytes 1048576 | tf_op jit(solution)/shard_map/all_to_all | solution.py:17
  60.8 0.8 copy.84
  61.6 11.5 %reduce.6 = bf16[2048,128]{1,0:T(8,128)(2,1)S(1)} reduce(bf16[2048,1,128]{2,1,0:T(2,128)(2,1)S(1)} %bitcast.150, bf16[]{:T(256)} %broadcast.69), dimensions={1}, to_apply=%bitcast.90.reduce_sub_computation | reduce | bytes 1048578
  73.1 0.9 reshape.183
  74.1 4.3 all-to-all-done
  78.4 8.0 %all-to-all-start.2 = ((bf16[16,2,8192]{2,1,0:T(2,128)(2,1)}), bf16[16,2,8192]{2,1,0:T(2,128)(2,1)S(1)}, u32[]{:S(2)}, u32[]{:S(2)}) async-start(bf16[16,2,8192]{2,1,0:T(2,128)(2,1)} %reshape.183), calls=%async_computation.2 | async-start | bytes 1048576 | tf_op jit(solution)/shard_map/all_to_all | solution.py:18
  86.5 0.5 reshape.188
  87.5 0.5 reshape.186
  88.4 15.7 %all-to-all-done.2 = bf16[16,2,8192]{2,1,0:T(2,128)(2,1)S(1)} async-done(((bf16[16,2,8192]{2,1,0:T(2,128)(2,1)}), bf16[16,2,8192]{2,1,0:T(2,128)(2,1)S(1)}, u32[]{:S(2)}, u32[]{:S(2)}) %all-to-all-start.2) | async-done | bytes 524320 | tf_op jit(solution)/shard_map/all_to_all | solution.py:18
  104.1 0.9 stack.2
  105.0 9.1 %all-to-all-start.4 = ((bf16[32,128,64]{1,2,0:T(8,128)(2,1)}), bf16[32,128,64]{1,2,0:T(8,128)(2,1)S(1)}, u32[]{:S(2)}, u32[]{:S(2)}) async-start(bf16[32,128,64]{1,2,0:T(8,128)(2,1)} %stack.2), calls=%async_computation.4 | async-start | bytes 1048576 | tf_op jit(solution)/shard_map/all_to_all | solution.py:66
  114.1 0.5 reshape.184
  115.0 3.1 gather_fusion.1
  118.1 3.0 gather_fusion
  121.1 5.8 %fusion.58 = (f32[32,64]{1,0:T(8,128)S(1)}, f32[32,64,512]{2,1,0:T(8,128)}) fusion(bf16[32,512,128]{2,1,0:T(8,128)(2,1)} %bitcast.143, bf16[32,64,128]{2,1,0:T(8,128)(2,1)S(1)} %bitcast.170), kind=kOutput, calls=%fused_computation.49 | convolution fusion | flops 271581696 | bytes 8921088 | tf_op jit(solution)/shard_map/sub | solution.py:54
  126.9 4.3 convolution_convert_fusion
  131.3 8.1 %copy.136 = bf16[1,2048,128]{2,0,1:T(2,128)(2,1)S(1)} copy(bf16[1,2048,128]{2,1,0:T(8,128)(2,1)S(1)} %bitcast.152) | data formatting | bytes 1048576 | tf_op jit(solution)/shard_map/reshape;transpose;reshape | solution.py:35
  139.4 11.7 %reduce.9 = bf16[2048,128]{1,0:T(8,128)(2,1)S(1)} reduce(bf16[2048,1,128]{2,1,0:T(2,128)(2,1)S(1)} %bitcast.151, bf16[]{:T(256)} %broadcast.69), dimensions={1}, to_apply=%bitcast.127.reduce_sub_computation | reduce | bytes 1048578
  151.2 0.9 reshape.189
  152.1 8.2 %all-to-all-start.3 = ((bf16[16,2,8192]{2,1,0:T(2,128)(2,1)}), bf16[16,2,8192]{2,1,0:T(2,128)(2,1)S(1)}, u32[]{:S(2)}, u32[]{:S(2)}) async-start(bf16[16,2,8192]{2,1,0:T(2,128)(2,1)} %reshape.189), calls=%async_computation.3 | async-start | bytes 1048576 | tf_op jit(solution)/shard_map/all_to_all | solution.py:64
  160.3 80.0 %all-gather.2.cloned.1.call-done = bf16[1,2048,2048]{2,1,0:T(8,128)(2,1)} async-done(((bf16[1,128,2048]{2,1,0:T(8,128)(2,1)}), bf16[1,2048,2048]{2,1,0:T(8,128)(2,1)}) %all-gather.2.cloned.1.call-update) | async-done | bytes 8388624 | tf_op jit(solution)/shard_map/all_gather | solution.py:68
  240.2 5.9 %fusion.18 = bf16[2048,128]{1,0:T(8,128)(2,1)S(1)} fusion(bf16[128,2048]{0,1:T(8,128)(2,1)S(1)} %bitcast.172, bf16[1,2048,2048]{2,1,0:T(8,128)(2,1)} %all-gather.2.cloned.1.call-done), kind=kOutput, calls=%fused_computation.22 | convolution fusion | flops 1074003968 | bytes 9437184 | tf_op jit(solution)/shard_map/dot_general | solution.py:69
  246.1 3.5 fusion.61
  249.7 18.6 %fusion.42 = bf16[32,64,128]{2,1,0:T(8,128)(2,1)S(1)} fusion(bf16[32,512,128]{2,1,0:T(8,128)(2,1)} %bitcast.144, f32[32,64,512]{2,1,0:T(8,128)} %fusion.61, f32[32,64,512]{2,1,0:T(8,128)} %get-tuple-element.26, f32[32,64]{1,0:T(8,128)S(1)} %get-tuple-element.25), kind=kOutput, calls=%fused_computation.34 | convolution fusion | flops 276040192 | bytes 13115392 | tf_op jit(solution)/shard_map/hbqk,hbkd->hbqd/dot_general | solution.py:96
  268.2 8.1 %copy.135 = bf16[1,2048,128]{2,0,1:T(2,128)(2,1)S(1)} copy(bf16[1,2048,128]{2,1,0:T(8,128)(2,1)S(1)} %bitcast.169) | data formatting | bytes 1048576 | tf_op jit(solution)/shard_map/reshape;transpose;reshape | solution.py:35
  276.4 12.0 %reduce.10 = bf16[2048,128]{1,0:T(8,128)(2,1)S(1)} reduce(bf16[2048,1,128]{2,1,0:T(2,128)(2,1)S(1)} %bitcast.147, bf16[]{:T(256)} %broadcast.69), dimensions={1}, to_apply=%bitcast.126.reduce_sub_computation | reduce | bytes 1048578
  288.4 0.9 reshape.191
  289.3 7.2 %all-to-all-start.5 = ((bf16[16,2,8192]{2,1,0:T(2,128)(2,1)}), bf16[16,2,8192]{2,1,0:T(2,128)(2,1)S(1)}, u32[]{:S(2)}, u32[]{:S(2)}) async-start(bf16[16,2,8192]{2,1,0:T(2,128)(2,1)} %reshape.191), calls=%async_computation.5 | async-start | bytes 1048576 | tf_op jit(solution)/shard_map/all_to_all | solution.py:121
  296.6 7.8 %fusion.2 = f32[128,2048]{0,1:T(8,128)} fusion(bf16[2048,128]{1,0:T(8,128)(2,1)S(1)} %bitcast.153, bf16[1,2048,2048]{2,1,0:T(8,128)(2,1)} %all-gather.2.cloned.1.call-done), kind=kOutput, calls=%fused_computation.6 | convolution fusion | flops 1073741824 | bytes 9961472 | tf_op jit(solution)/shard_map/dot_general | solution.py:72
  304.4 20.8 %fusion.22 = f32[32,512,128]{2,1,0:T(8,128)} fusion(bf16[32,64,128]{2,1,0:T(8,128)(2,1)S(1)} %bitcast.171, f32[32,64,512]{2,1,0:T(8,128)} %fusion.61, f32[32,64,512]{2,1,0:T(8,128)} %get-tuple-element.26, f32[32,64]{1,0:T(8,128)S(1)} %get-tuple-element.25), kind=kOutput, calls=%fused_computation.23 | convolution fusion | flops 275778048 | bytes 17309696 | tf_op jit(solution)/shard_map/hbqk,hbqd->hbkd/dot_general | solution.py:99
  325.2 9.6 %reshape.150 = f32[32,8,8192]{2,1,0:T(8,128)} reshape(f32[32,512,128]{2,1,0:T(8,128)} %fusion.22) | data formatting | bytes 16777216 | tf_op jit(solution)/shard_map/reshape.36
  334.8 5.1 %copy.132 = f32[32,8,64,128]{3,2,1,0:T(8,128)S(1)} copy(f32[32,8,64,128]{3,1,2,0:T(8,128)} %bitcast.130) | data formatting | bytes 16777216
  339.9 8.2 %fusion.39 = bf16[32,64,128]{2,0,1:T(8,128)(2,1)S(1)} fusion(f32[64,128,32,8]{1,0,3,2:T(8,128)S(1)} %bitcast.131, s32[32,8]{0,1:T(8,128)S(1)} %bitcast.173), kind=kOutput, calls=%fused_computation.32 | convolution fusion | flops 805576704 | bytes 8913920 | tf_op jit(solution)/shard_map/hqsx,qsk->hkx/dot_general | solution.py:108
  348.3 8.3 %copy.134 = bf16[1,2048,128]{2,0,1:T(2,128)(2,1)S(1)} copy(bf16[1,2048,128]{2,1,0:T(8,128)(2,1)S(1)} %bitcast.157) | data formatting | bytes 1048576 | tf_op jit(solution)/shard_map/reshape;transpose;reshape | solution.py:35
  356.6 11.5 %reduce.11 = bf16[2048,128]{1,0:T(8,128)(2,1)S(1)} reduce(bf16[2048,1,128]{2,1,0:T(2,128)(2,1)S(1)} %bitcast.148, bf16[]{:T(256)} %broadcast.69), dimensions={1}, to_apply=%bitcast.125.reduce_sub_computation | reduce | bytes 1048578
  368.2 0.9 reshape.193
  369.1 8.6 %all-to-all-start.6 = ((bf16[16,2,8192]{2,1,0:T(2,128)(2,1)}), bf16[16,2,8192]{2,1,0:T(2,128)(2,1)S(1)}, u32[]{:S(2)}, u32[]{:S(2)}) async-start(bf16[16,2,8192]{2,1,0:T(2,128)(2,1)} %reshape.193), calls=%async_computation.6 | async-start | bytes 1048576 | tf_op jit(solution)/shard_map/all_to_all | solution.py:122
  377.7 7.2 %fusion.45 = f32[32,512,128]{2,1,0:T(8,128)} fusion(bf16[32,64,128]{2,1,0:T(8,128)(2,1)S(1)} %bitcast.168, f32[32,64,512]{2,1,0:T(8,128)} %get-tuple-element.26, f32[32,64]{1,0:T(8,128)S(1)} %get-tuple-element.25), kind=kOutput, calls=%fused_computation.35 | convolution fusion | flops 270532608 | bytes 13115392 | tf_op jit(solution)/shard_map/hbqk,hbqd->hbkd/dot_general | solution.py:80
  384.9 9.4 %reshape.151 = f32[32,8,8192]{2,1,0:T(8,128)} reshape(f32[32,512,128]{2,1,0:T(8,128)} %fusion.45) | data formatting | bytes 16777216 | tf_op jit(solution)/shard_map/reshape.43
  394.3 5.0 %copy.131 = f32[32,8,64,128]{3,2,1,0:T(8,128)S(1)} copy(f32[32,8,64,128]{3,1,2,0:T(8,128)} %bitcast.132) | data formatting | bytes 16777216
  399.3 8.2 %fusion.36 = bf16[32,64,128]{2,0,1:T(8,128)(2,1)S(1)} fusion(f32[64,128,32,8]{1,0,3,2:T(8,128)S(1)} %bitcast.133, s32[32,8]{0,1:T(8,128)S(1)} %bitcast.174), kind=kOutput, calls=%fused_computation.31 | convolution fusion | flops 805576704 | bytes 8913920 | tf_op jit(solution)/shard_map/hqsx,qsk->hkx/dot_general | solution.py:108
  407.7 8.3 %copy.133 = bf16[1,2048,128]{2,0,1:T(2,128)(2,1)S(1)} copy(bf16[1,2048,128]{2,1,0:T(8,128)(2,1)S(1)} %bitcast.158) | data formatting | bytes 1048576 | tf_op jit(solution)/shard_map/reshape;transpose;reshape | solution.py:35
  416.0 11.5 %reduce.12 = bf16[2048,128]{1,0:T(8,128)(2,1)S(1)} reduce(bf16[2048,1,128]{2,1,0:T(2,128)(2,1)S(1)} %bitcast.146, bf16[]{:T(256)} %broadcast.69), dimensions={1}, to_apply=%bitcast.124.reduce_sub_computation | reduce | bytes 1048578
  427.5 0.9 reshape.195
  428.5 8.1 %all-to-all-start.7 = ((bf16[16,2,8192]{2,1,0:T(2,128)(2,1)}), bf16[16,2,8192]{2,1,0:T(2,128)(2,1)S(1)}, u32[]{:S(2)}, u32[]{:S(2)}) async-start(bf16[16,2,8192]{2,1,0:T(2,128)(2,1)} %reshape.195), calls=%async_computation.7 | async-start | bytes 1048576 | tf_op jit(solution)/shard_map/all_to_all | solution.py:123
  436.6 0.5 reshape.190
  437.5 1.0 copy.98
  438.5 0.5 reshape.192
  439.4 1.0 copy.99
  440.4 0.5 reshape.194
  441.3 1.0 copy.100
  442.3 9.7 %all-to-all-done.7 = bf16[16,2,8192]{2,1,0:T(2,128)(2,1)S(1)} async-done(((bf16[16,2,8192]{2,1,0:T(2,128)(2,1)}), bf16[16,2,8192]{2,1,0:T(2,128)(2,1)S(1)}, u32[]{:S(2)}, u32[]{:S(2)}) %all-to-all-start.7) | async-done | bytes 524320 | tf_op jit(solution)/shard_map/all_to_all | solution.py:123
  452.0 0.5 reshape.196
  452.9 1.0 copy.101
  (42 shorter events, 3.2 us)
Async XLA Ops:
  7.2 27.9 %copy-start.1 = (bf16[1,128,2048]{2,1,0:T(8,128)(2,1)S(1)}, bf16[1,128,2048]{2,1,0:T(8,128)(2,1)}, u32[]{:S(2)}) copy-start(bf16[1,128,2048]{2,1,0:T(8,128)(2,1)} %param.7) | copy-start | bytes 1572868
  7.2 233.1 %all-gather.2.cloned.1.call-start = ((), (), s32[]{:S(2)}) async-start(), calls=%async_computation.9 | async-start | bytes 8912896 | tf_op jit(solution)/shard_map/all_gather | solution.py:68
  10.8 50.1 %copy-start.2 = (bf16[1,128,2048]{2,1,0:T(8,128)(2,1)S(1)}, bf16[1,128,2048]{2,1,0:T(8,128)(2,1)}, u32[]{:S(2)}) copy-start(bf16[1,128,2048]{2,1,0:T(8,128)(2,1)} %param.8) | copy-start | bytes 1572868
  23.3 27.8 %all-to-all-start.1 = ((bf16[16,2,8192]{2,1,0:T(2,128)(2,1)}), bf16[16,2,8192]{2,1,0:T(2,128)(2,1)S(1)}, u32[]{:S(2)}, u32[]{:S(2)}) async-start(bf16[16,2,8192]{2,1,0:T(2,128)(2,1)} %reshape.187), calls=%async_computation.1 | async-start | bytes 1048576 | tf_op jit(solution)/shard_map/all_to_all | solution.py:16
  35.8 50.5 %copy-start.5 = (s32[1,32,8]{1,2,0:T(8,128)S(1)}, s32[1,32,8]{1,2,0:T(8,128)}, u32[]{:S(2)}) copy-start(s32[1,32,8]{1,2,0:T(8,128)} %param.11) | copy-start | bytes 3076
  51.1 27.2 %all-to-all-start = ((bf16[16,2,8192]{2,1,0:T(2,128)(2,1)}), bf16[16,2,8192]{2,1,0:T(2,128)(2,1)S(1)}, u32[]{:S(2)}, u32[]{:S(2)}) async-start(bf16[16,2,8192]{2,1,0:T(2,128)(2,1)} %reshape.185), calls=%async_computation | async-start | bytes 1048576 | tf_op jit(solution)/shard_map/all_to_all | solution.py:17
  78.4 25.7 %all-to-all-start.2 = ((bf16[16,2,8192]{2,1,0:T(2,128)(2,1)}), bf16[16,2,8192]{2,1,0:T(2,128)(2,1)S(1)}, u32[]{:S(2)}, u32[]{:S(2)}) async-start(bf16[16,2,8192]{2,1,0:T(2,128)(2,1)} %reshape.183), calls=%async_computation.2 | async-start | bytes 1048576 | tf_op jit(solution)/shard_map/all_to_all | solution.py:18
  86.5 17.5 %copy-start.6 = (bf16[128,64]{0,1:T(8,128)(2,1)S(1)}, bf16[128,64]{0,1:T(8,128)(2,1)}, u32[]{:S(2)}) copy-start(bf16[128,64]{0,1:T(8,128)(2,1)} %param.9) | copy-start | bytes 49156
  87.4 33.7 %copy-start.3 = (bf16[1,16,128,128]{3,2,1,0:T(8,128)(2,1)}, bf16[1,16,128,128]{3,2,1,0:T(8,128)(2,1)S(1)}, u32[]{:S(2)}) copy-start(bf16[1,16,128,128]{3,2,1,0:T(8,128)(2,1)S(1)} %copy.83) | copy-start | bytes 1572868
  105.0 47.1 %all-to-all-start.4 = ((bf16[32,128,64]{1,2,0:T(8,128)(2,1)}), bf16[32,128,64]{1,2,0:T(8,128)(2,1)S(1)}, u32[]{:S(2)}, u32[]{:S(2)}) async-start(bf16[32,128,64]{1,2,0:T(8,128)(2,1)} %stack.2), calls=%async_computation.4 | async-start | bytes 1048576 | tf_op jit(solution)/shard_map/all_to_all | solution.py:66
  152.1 137.2 %all-to-all-start.3 = ((bf16[16,2,8192]{2,1,0:T(2,128)(2,1)}), bf16[16,2,8192]{2,1,0:T(2,128)(2,1)S(1)}, u32[]{:S(2)}, u32[]{:S(2)}) async-start(bf16[16,2,8192]{2,1,0:T(2,128)(2,1)} %reshape.189), calls=%async_computation.3 | async-start | bytes 1048576 | tf_op jit(solution)/shard_map/all_to_all | solution.py:64
  240.2 5.9 %copy-start = (bf16[256,64,128]{2,1,0:T(8,128)(2,1)S(1)}, bf16[256,64,128]{2,1,0:T(8,128)(2,1)}, u32[]{:S(2)}) copy-start(bf16[256,64,128]{2,1,0:T(8,128)(2,1)} %gather_fusion.1) | copy-start | bytes 12582916
  289.3 79.8 %all-to-all-start.5 = ((bf16[16,2,8192]{2,1,0:T(2,128)(2,1)}), bf16[16,2,8192]{2,1,0:T(2,128)(2,1)S(1)}, u32[]{:S(2)}, u32[]{:S(2)}) async-start(bf16[16,2,8192]{2,1,0:T(2,128)(2,1)} %reshape.191), calls=%async_computation.5 | async-start | bytes 1048576 | tf_op jit(solution)/shard_map/all_to_all | solution.py:121
  296.5 157.4 %reduce-scatter.2.cloned.1.call-start = ((), (), s32[]{:S(2)}) async-start(), calls=%async_computation.10 | async-start | bytes 1081344 | tf_op jit(solution)/shard_map/reduce_scatter | solution.py:11
  296.6 7.8 %copy-start.4 = (bf16[1,16,128,128]{3,2,1,0:T(8,128)(2,1)S(1)}, bf16[1,16,128,128]{3,2,1,0:T(8,128)(2,1)}, u32[]{:S(2)}) copy-start(bf16[1,16,128,128]{3,2,1,0:T(8,128)(2,1)} %copy-done.3) | copy-start | bytes 1572868
  369.1 59.4 %all-to-all-start.6 = ((bf16[16,2,8192]{2,1,0:T(2,128)(2,1)}), bf16[16,2,8192]{2,1,0:T(2,128)(2,1)S(1)}, u32[]{:S(2)}, u32[]{:S(2)}) async-start(bf16[16,2,8192]{2,1,0:T(2,128)(2,1)} %reshape.193), calls=%async_computation.6 | async-start | bytes 1048576 | tf_op jit(solution)/shard_map/all_to_all | solution.py:122
  428.5 23.6 %all-to-all-start.7 = ((bf16[16,2,8192]{2,1,0:T(2,128)(2,1)}), bf16[16,2,8192]{2,1,0:T(2,128)(2,1)S(1)}, u32[]{:S(2)}, u32[]{:S(2)}) async-start(bf16[16,2,8192]{2,1,0:T(2,128)(2,1)} %reshape.195), calls=%async_computation.7 | async-start | bytes 1048576 | tf_op jit(solution)/shard_map/all_to_all | solution.py:123
Sparse Core Ops, SparseCore 0:
  10.1 230.1 all-gather.1
  304.5 93.6 reduce-scatter.1
